TPU v7x, 32 devices: a whole 2x2x4 slice. The times are simulated.
32 devices in a mesh: groups: 2 (over y), roll: 4 (over z), tp: 2 (over x), seq: 2 (over core).
Axes of the slice: x: 2, y: 2, z: 4, core: 2. Of those that a mesh axis runs over, the one named last changes fastest.
Arguments:
- hidden: bfloat16 [128, 8192], P('groups', ('roll', 'seq')), parts along dimension 0, may hold values from -6 to 6
- w_query: bfloat16 [8192, 8192], P(('roll', 'seq'), 'tp'), may hold values from -0.0625 to 0.0625
- w_key: bfloat16 [8192, 1024], P(('roll', 'seq'), 'tp'), may hold values from -0.0625 to 0.0625
- w_value: bfloat16 [8192, 1024], P(('roll', 'seq'), 'tp'), may hold values from -0.0625 to 0.0625
- b_query: bfloat16 [8192], P('tp'), may hold values from -12 to 12
- b_key: bfloat16 [1024], P('tp'), may hold values from -12 to 12
- b_value: bfloat16 [1024], P('tp'), may hold values from -6 to 6
- w_out: bfloat16 [8192, 8192], P('tp', ('roll', 'seq')), may hold values from -0.0625 to 0.0625
- prefix_keys: bfloat16 [4, 4096, 1024], P('groups', ('roll', 'seq'), 'tp'), parts along dimension 0, may hold values from -256 to 256
- prefix_values: bfloat16 [4, 4096, 1024], P('groups', ('roll', 'seq'), 'tp'), parts along dimension 0, may hold values from -6 to 6
- suffix_keys: bfloat16 [16, 2048, 1024], P(('groups', 'roll'), 'seq', 'tp'), parts along dimension 0, may hold values from -6 to 6
- suffix_values: bfloat16 [16, 2048, 1024], P(('groups', 'roll'), 'seq', 'tp'), parts along dimension 0, may hold values from -6 to 6
- suffix_lengths: int32 [16], P('groups'), parts along dimension 0, may hold values from 1 to 2048, 8192 in all
- prompt_of: int32 [16], P('groups'), parts along dimension 0, may hold values from 0 to 1, as said below
Outputs:
- attended: bfloat16 [128, 8192], P(('groups', 'tp'), ('roll', 'seq')), parts along dimension 0
There are 2 independent parts, one for each index of `groups`. A program takes and returns all parts, laid end to end along the dimension named above; an argument that names none is the same for every part. Nothing has to cross between parts.
Inputs may be any that keep to these rules, and one draw needn't show every extreme that they name: Only the first suffix_lengths[r] rows of a rollout's suffix cache are live; the lengths of a group add up to 8192 and the largest is exactly 2048. `prompt_of`: every prompt is extended by exactly 4 rollouts.
All inputs are finite; a program needn't handle non-finite values.
Results may differ from a plain program's by a relative error of at most 0.009.
The roundings to bfloat16 on the way count: a program that leaves them out, or rounds other values in their place, can miss the bound.
Values may be sent and summed in bfloat16 or wider, within the bound.
A program may use at most 128 MiB of HBM per device.

v0:
```python
import math

import jax
import jax.numpy as jnp
from jax import lax
from jax.sharding import PartitionSpec as P

HD = 128
GUESS = 8


ROPE_BASE = 1000000.0
NEG_FILL = -1e30


def rotate(values, positions):
    half = values.shape[-1] // 2
    steps = jnp.arange(half).astype(jnp.float32) * (2.0 / values.shape[-1])
    freqs = jnp.exp(-math.log(ROPE_BASE) * steps)
    angles = positions[:, None] * freqs[None, :]
    cosine = jnp.cos(angles)[:, None, :]
    sine = jnp.sin(angles)[:, None, :]
    first = values[..., :half]
    second = values[..., half:]
    return jnp.concatenate(
        [first * cosine - second * sine, second * cosine + first * sine], axis=-1
    )


def lookup(table, indices):
    hits = indices[:, None] == jnp.arange(table.shape[0], dtype=jnp.int32)[None, :]
    return jnp.sum(jnp.where(hits, table[None, :], 0), axis=1)


def combine(first, second):
    peak_a, total_a, numer_a = first
    peak_b, total_b, numer_b = second
    peak = jnp.maximum(peak_a, peak_b)
    factor_a = jnp.exp(peak_a - peak)
    factor_b = jnp.exp(peak_b - peak)
    return (
        peak,
        total_a * factor_a + total_b * factor_b,
        numer_a * factor_a[..., None] + numer_b * factor_b[..., None],
    )


def masked_stats(scores, visible, values):
    peak = jnp.max(jnp.where(visible, scores, NEG_FILL), axis=-1)
    weights = jnp.exp(jnp.where(visible, scores - peak[..., None], NEG_FILL))
    total = jnp.sum(weights, axis=-1)
    numer = jnp.einsum(
        "rtkgs,rskd->rtkgd",
        weights.astype(jnp.bfloat16),
        values,
        preferred_element_type=jnp.float32,
    )
    return (peak, total, numer)


def body(
    hidden,
    w_query,
    w_key,
    w_value,
    b_query,
    b_key,
    b_value,
    w_out,
    prefix_keys,
    prefix_values,
    suffix_keys,
    suffix_values,
    suffix_lengths,
    prompt_of,
):
    row_count = hidden.shape[0]
    q_heads = w_query.shape[1] // HD
    kv_heads = w_key.shape[1] // HD
    group = q_heads // kv_heads
    prompts = prefix_keys.shape[0]
    pre_dev = prefix_keys.shape[1]
    prefix_total = pre_dev * lax.axis_size(("roll", "seq"))
    per_device = suffix_keys.shape[0]
    suf_dev = suffix_keys.shape[1]
    scale = 1.0 / math.sqrt(HD)
    q_part = jnp.dot(hidden, w_query, preferred_element_type=jnp.float32)
    k_part = jnp.dot(hidden, w_key, preferred_element_type=jnp.float32)
    v_part = jnp.dot(hidden, w_value, preferred_element_type=jnp.float32)
    q_sum, k_sum, v_sum = lax.psum((q_part, k_part, v_part), ("roll", "seq"))
    count = q_sum.shape[0]
    row_ids = jnp.arange(count, dtype=jnp.int32)
    owner_ids = row_ids // GUESS
    positions = (prefix_total + lookup(suffix_lengths, owner_ids) + row_ids % GUESS).astype(
        jnp.float32
    )
    q_rot = rotate((q_sum + b_query.astype(jnp.float32)).reshape(count, q_heads, HD), positions)
    k_rot = rotate((k_sum + b_key.astype(jnp.float32)).reshape(count, kv_heads, HD), positions)
    v_fin = (v_sum + b_value.astype(jnp.float32)).reshape(count, kv_heads, HD)
    query = q_rot.astype(jnp.bfloat16)
    key_new = k_rot.astype(jnp.bfloat16)
    value_new = v_fin.astype(jnp.bfloat16)
    query_grid = query.reshape(row_count, kv_heads, group, HD)
    owners_all = jnp.arange(row_count, dtype=jnp.int32) // GUESS
    row_prompt = lookup(prompt_of, owners_all)
    pre_keys = prefix_keys.reshape(prompts, pre_dev, kv_heads, HD)
    pre_values = prefix_values.reshape(prompts, pre_dev, kv_heads, HD)
    peak_all = jnp.full((row_count, kv_heads, group), NEG_FILL, jnp.float32)
    total_all = jnp.zeros((row_count, kv_heads, group), jnp.float32)
    numer_all = jnp.zeros((row_count, kv_heads, group, HD), jnp.float32)
    for prompt in range(prompts):
        scores = (
            jnp.einsum(
                "tkgd,skd->tkgs", query_grid, pre_keys[prompt], preferred_element_type=jnp.float32
            )
            * scale
        )
        block_peak = jnp.max(scores, axis=-1)
        weights = jnp.exp(scores - block_peak[..., None])
        block_numer = jnp.einsum(
            "tkgs,skd->tkgd",
            weights.astype(jnp.bfloat16),
            pre_values[prompt],
            preferred_element_type=jnp.float32,
        )
        picked = (row_prompt == prompt)[:, None, None]
        peak_all = jnp.where(picked, block_peak, peak_all)
        total_all = jnp.where(picked, jnp.sum(weights, axis=-1), total_all)
        numer_all = jnp.where(picked[..., None], block_numer, numer_all)
    first_rollout = lax.axis_index("roll") * per_device
    seq_index = lax.axis_index("seq")
    local_len = lax.dynamic_slice_in_dim(suffix_lengths, first_rollout, per_device, 0)
    live = jnp.clip(local_len - seq_index * suf_dev, 0, suf_dev)
    row_start = first_rollout * GUESS
    local_rows = per_device * GUESS
    query_local = lax.dynamic_slice_in_dim(query_grid, row_start, local_rows, 0).reshape(
        per_device, GUESS, kv_heads, group, HD
    )
    suf_keys = suffix_keys.reshape(per_device, suf_dev, kv_heads, HD)
    suf_values = suffix_values.reshape(per_device, suf_dev, kv_heads, HD)
    scores = (
        jnp.einsum("rtkgd,rskd->rtkgs", query_local, suf_keys, preferred_element_type=jnp.float32)
        * scale
    )
    visible = (jnp.arange(suf_dev, dtype=jnp.int32)[None, :] < live[:, None])[
        :, None, None, None, :
    ]
    suffix_part = masked_stats(scores, visible, suf_values)
    key_local = lax.dynamic_slice_in_dim(key_new, row_start, local_rows, 0).reshape(
        per_device, GUESS, kv_heads, HD
    )
    value_local = lax.dynamic_slice_in_dim(value_new, row_start, local_rows, 0).reshape(
        per_device, GUESS, kv_heads, HD
    )
    new_scores = (
        jnp.einsum("rtkgd,rskd->rtkgs", query_local, key_local, preferred_element_type=jnp.float32)
        * scale
    )
    guess_ids = jnp.arange(GUESS, dtype=jnp.int32)
    causal = (guess_ids[None, :] <= guess_ids[:, None]) & (seq_index == 0)
    guess_part = masked_stats(new_scores, causal[None, :, None, None, :], value_local)
    prefix_local = (
        lax.dynamic_slice_in_dim(peak_all, row_start, local_rows, 0).reshape(
            per_device, GUESS, kv_heads, group
        ),
        lax.dynamic_slice_in_dim(total_all, row_start, local_rows, 0).reshape(
            per_device, GUESS, kv_heads, group
        ),
        lax.dynamic_slice_in_dim(numer_all, row_start, local_rows, 0).reshape(
            per_device, GUESS, kv_heads, group, HD
        ),
    )
    peak_loc, total_loc, numer_loc = combine(combine(prefix_local, suffix_part), guess_part)
    peak_all = lax.dynamic_update_slice_in_dim(
        peak_all, peak_loc.reshape(local_rows, kv_heads, group), row_start, 0
    )
    total_all = lax.dynamic_update_slice_in_dim(
        total_all, total_loc.reshape(local_rows, kv_heads, group), row_start, 0
    )
    numer_all = lax.dynamic_update_slice_in_dim(
        numer_all, numer_loc.reshape(local_rows, kv_heads, group, HD), row_start, 0
    )
    peaks, totals, numers = (
        lax.all_to_all(peak_all[None], ("roll", "seq"), split_axis=1, concat_axis=0, tiled=True),
        lax.all_to_all(total_all[None], ("roll", "seq"), split_axis=1, concat_axis=0, tiled=True),
        lax.all_to_all(numer_all[None], ("roll", "seq"), split_axis=1, concat_axis=0, tiled=True),
    )
    peak_top = jnp.max(peaks, axis=0)
    factors = jnp.exp(peaks - peak_top[None])
    share = (
        jnp.sum(numers * factors[..., None], axis=0) / jnp.sum(totals * factors, axis=0)[..., None]
    )
    share = share.astype(jnp.bfloat16).reshape(share.shape[0], q_heads * HD)
    attention = lax.all_gather(share, ("roll", "seq"), axis=0, tiled=True)
    summed = lax.psum_scatter(
        jnp.dot(attention, w_out, preferred_element_type=jnp.float32),
        "tp",
        scatter_dimension=0,
        tiled=True,
    )
    return summed.astype(jnp.bfloat16)


def solution(mesh):
    return jax.shard_map(
        body,
        mesh=mesh,
        in_specs=(
            P("groups", ("roll", "seq")),
            P(("roll", "seq"), "tp"),
            P(("roll", "seq"), "tp"),
            P(("roll", "seq"), "tp"),
            P("tp"),
            P("tp"),
            P("tp"),
            P("tp", ("roll", "seq")),
            P("groups", ("roll", "seq"), "tp"),
            P("groups", ("roll", "seq"), "tp"),
            P(("groups", "roll"), "seq", "tp"),
            P(("groups", "roll"), "seq", "tp"),
            P("groups"),
            P("groups"),
        ),
        out_specs=P(("groups", "tp"), ("roll", "seq")),
        check_vma=False,
    )
```

profile of v0, /device:TPU:0, one launch (start us, length us, event | category | flops | bytes accessed | tf_op | source)
XLA Modules:
  0.0 187.7 jit_solution(5365839674309538938)
XLA Ops:
  6.6 6.2 %fusion.91 = f32[64,4096]{1,0:T(8,128)} fusion(bf16[64,1024]{1,0:T(8,128)(2,1)} %param.14, bf16[1024,4096]{1,0:T(8,128)(2,1)} %param.15), kind=kOutput, calls=%fused_computation.143 | convolution fusion | flops 536870912 | bytes 9568256 | tf_op jit(solution)/shard_map/dot_general | solution.py:87
  12.8 1.0 fusion.92
  13.8 0.9 fusion.93
  15.5 4.0 %reshape.290 = bf16[2,1024,4,128]{3,2,1,0:T(4,128)(2,1)} reshape(bf16[2,1024,512]{2,1,0:T(8,128)(2,1)} %param.24) | data formatting | bytes 4194304 | tf_op jit(solution)/shard_map/reshape | solution.py:139
  19.5 0.6 dynamic-slice.4
  20.2 0.6 dynamic-slice.5
  20.8 1.3 fusion.89
  22.0 1.0 copy.245
  23.1 1.0 copy.243
  24.1 4.0 %reshape.291 = bf16[2,1024,4,128]{3,2,1,0:T(4,128)(2,1)} reshape(bf16[2,1024,512]{2,1,0:T(8,128)(2,1)} %param.25) | data formatting | bytes 4194304 | tf_op jit(solution)/shard_map/reshape | solution.py:140
  28.5 49.6 %all-reduce.3.cloned.1.call-done = (f32[64,4096]{1,0:T(8,128)}, f32[64,512]{1,0:T(8,128)}, f32[64,512]{1,0:T(8,128)}) async-done(((f32[64,4096]{1,0:T(8,128)}, f32[64,512]{1,0:T(8,128)}, f32[64,512]{1,0:T(8,128)}), (f32[64,4096]{1,0:T(8,128)}, f32[64,512]{1,0:T(8,128)}, f32[64,512]{1,0:T(8,128)})) %all-reduce.3.cloned.1.call-update) | async-done | bytes 1310736 | tf_op jit(solution)/shard_map/psum | solution.py:90
  78.0 1.3 add_bitcast_fusion
  79.8 0.5 fusion.50
  80.4 0.9 bitcast_reduce_fusion.1
  81.3 0.9 bitcast_reduce_fusion
  82.2 0.7 select_reduce_fusion
  83.1 1.1 copy-done.6
  84.2 2.3 %fusion.2 = (f32[64,4,8]{2,0,1:T(8,128)S(1)}, f32[64,4,8]{2,0,1:T(8,128)S(1)}) fusion(f32[4,64,8,512]{3,2,1,0:T(8,128)S(1)} %get-tuple-element.37, f32[64,4,8]{2,0,1:T(8,128)S(1)} %get-tuple-element.36, f32[64,4,8]{2,0,1:T(8,128)S(1)} %get-tuple-element.34, f32[4,64,8,512]{3,2,1,0:T(8,128)S(1)} %get-tuple-element.35), kind=kLoop, calls=%fused_computation.6 | loop fusion | flops 6287360 | bytes 8421376 | tf_op jit(solution)/shard_map/reduce_sum | solution.py:128
  86.7 0.9 fusion.12
  87.7 0.6 fusion.21
  88.4 0.7 fusion.63
  89.1 0.7 copy.324
  89.8 1.7 reshape.303
  91.5 3.5 %all-to-all-start.1 = ((f32[8,1,256]{2,1,0:T(1,128)}), f32[8,1,256]{2,1,0:T(1,128)S(1)}, u32[]{:S(2)}, u32[]{:S(2)}) async-start(f32[8,1,256]{2,1,0:T(1,128)} %reshape.303), calls=%async_computation.1 | async-start | bytes 16384 | tf_op jit(solution)/shard_map/all_to_all | solution.py:184
  95.0 3.2 %fusion.26 = f32[4,64,8,128]{3,2,1,0:T(8,128)S(1)} fusion(bf16[512,4,128,1]{0,2,3,1:T(8,128)(2,1)} %bitcast.189, f32[4,64,8,512]{3,2,1,0:T(8,128)} %copy-done.3, f32[64,4,8]{2,0,1:T(8,128)S(1)} %get-tuple-element.34, pred[64]{0:T(512)(128)(4,1)} %copy-done.20), kind=kOutput, calls=%fused_computation.28 | convolution fusion | flops 271843328 | bytes 5775424 | tf_op jit(solution)/shard_map/tkgs,skd->tkgd/dot_general | solution.py:120
  98.1 0.4 copy-done.2
  98.7 1.6 fusion.23
  100.2 1.0 copy-done.5
  101.2 0.7 constant_dynamic-slice_fusion.2
  101.9 0.6 convert_element_type.64
  102.6 0.8 constant_dynamic-slice_fusion
  103.3 2.6 %fusion.41 = f32[2,8,4,8,128]{4,3,1,2,0:T(8,128)S(1)} fusion(bf16[2,1024,4,128,1]{3,2,1,0,4:T(4,128)(2,1)} %bitcast.192, f32[2,4,8,8,1024]{4,3,2,1,0:T(8,128)S(1)} %get-tuple-element.39, f32[2,8,4,8]{3,1,2,0:T(8,128)S(1)} %get-tuple-element.38, pred[2,1024]{1,0:T(4,128)(4,1)S(1)} %iota_compare_fusion, f32[2,8,4,8,128]{4,3,1,0,2:T(8,128)} %bitcast.202, ...), kind=kOutput, calls=%fused_computation.37 | convolution fusion | flops 136577024 | bytes 4728832 | tf_op jit(solution)/shard_map/rtkgs,rskd->rtkgd/dot_general | solution.py:52
  106.0 0.3 fusion.34
  106.4 0.8 reshape.305
  107.2 4.9 %all-to-all-start.2 = ((f32[8,1,256]{2,1,0:T(1,128)}), f32[8,1,256]{2,1,0:T(1,128)S(1)}, u32[]{:S(2)}, u32[]{:S(2)}) async-start(f32[8,1,256]{2,1,0:T(1,128)} %reshape.305), calls=%async_computation.2 | async-start | bytes 16384 | tf_op jit(solution)/shard_map/all_to_all | solution.py:185
  112.0 0.7 constant_dynamic-update-slice_fusion
  112.8 2.4 %copy.197 = f32[1,64,4,8,128]{4,3,2,0,1:T(8,128)} copy(f32[1,64,4,8,128]{4,3,1,2,0:T(8,128)} %constant_dynamic-update-slice_fusion) | data formatting | bytes 2097152 | tf_op jit(solution)/shard_map/dynamic_update_slice | solution.py:180
  115.2 2.5 %all-to-all-done.2 = f32[8,1,256]{2,1,0:T(1,128)S(1)} async-done(((f32[8,1,256]{2,1,0:T(1,128)}), f32[8,1,256]{2,1,0:T(1,128)S(1)}, u32[]{:S(2)}, u32[]{:S(2)}) %all-to-all-start.2) | async-done | bytes 8224 | tf_op jit(solution)/shard_map/all_to_all | solution.py:185
  117.7 3.6 %all-to-all-start = ((f32[1,64,4,8,128]{4,3,2,0,1:T(8,128)}), f32[1,64,4,8,128]{4,3,2,0,1:T(8,128)S(1)}, u32[]{:S(2)}, u32[]{:S(2)}) async-start(f32[1,64,4,8,128]{4,3,2,0,1:T(8,128)} %copy.197), calls=%async_computation | async-start | bytes 2097152 | tf_op jit(solution)/shard_map/all_to_all | solution.py:186
  121.3 0.5 broadcast.227
  121.8 0.7 reduce.1
  122.9 0.7 reduce
  124.2 23.6 %all-to-all-done = f32[1,64,4,8,128]{4,3,2,0,1:T(8,128)S(1)} async-done(((f32[1,64,4,8,128]{4,3,2,0,1:T(8,128)}), f32[1,64,4,8,128]{4,3,2,0,1:T(8,128)S(1)}, u32[]{:S(2)}, u32[]{:S(2)}) %all-to-all-start) | async-done | bytes 1048608 | tf_op jit(solution)/shard_map/all_to_all | solution.py:186
  147.7 0.3 fusion.45
  148.2 14.9 %all_gather.3 = bf16[64,4096]{1,0:T(8,128)(2,1)S(1)} all-gather(bf16[8,4096]{1,0:T(8,128)(2,1)S(1)} %bitcast.203), channel_id=1, replica_groups=mesh['groups'=2,'roll'=4,'tp'=2,'seq'=2] {'roll','seq'}, dimensions={0}, use_global_device_ids=true | all-gather | bytes 589824 | tf_op jit(solution)/shard_map/all_gather | solution.py:194
  163.2 5.7 %fusion.94 = f32[64,1024]{1,0:T(8,128)} fusion(bf16[64,4096]{1,0:T(8,128)(2,1)S(1)} %all_gather.3, bf16[4096,1024]{1,0:T(8,128)(2,1)} %param.21), kind=kOutput, calls=%fused_computation.146 | convolution fusion | flops 536870912 | bytes 9175040 | tf_op jit(solution)/shard_map/dot_general | solution.py:196
  168.9 10.4 %reduce-scatter.2.cloned.1.call-done = f32[32,1024]{1,0:T(8,128)} async-done(((f32[64,1024]{1,0:T(8,128)}), f32[32,1024]{1,0:T(8,128)}) %reduce-scatter.2.cloned.1.call-update) | async-done | bytes 131088 | tf_op jit(solution)/shard_map/reduce_scatter | solution.py:195
  179.3 1.5 convert_element_type.68
  (96 shorter events, 3.5 us)
Async XLA Ops:
  6.5 6.3 %copy-start = (bf16[1024,512]{1,0:T(8,128)(2,1)S(1)}, bf16[1024,512]{1,0:T(8,128)(2,1)}, u32[]{:S(2)}) copy-start(bf16[1024,512]{1,0:T(8,128)(2,1)} %param.16) | copy-start | bytes 3145732
  6.5 6.3 %copy-start.9 = (bf16[64,1024]{1,0:T(8,128)(2,1)S(1)}, bf16[64,1024]{1,0:T(8,128)(2,1)}, u32[]{:S(2)}) copy-start(bf16[64,1024]{1,0:T(8,128)(2,1)} %param.14) | copy-start | bytes 393220
  6.5 7.2 %copy-start.10 = (bf16[1024,512]{1,0:T(8,128)(2,1)S(1)}, bf16[1024,512]{1,0:T(8,128)(2,1)}, u32[]{:S(2)}) copy-start(bf16[1024,512]{1,0:T(8,128)(2,1)} %param.17) | copy-start | bytes 3145732
  6.5 8.2 %copy-start.17 = (bf16[4096]{0:T(1024)(128)(2,1)S(1)}, bf16[4096]{0:T(1024)(128)(2,1)}, u32[]{:S(2)}) copy-start(bf16[4096]{0:T(1024)(128)(2,1)} %param.18) | copy-start | bytes 24580
  6.5 8.3 %copy-start.23 = (bf16[512]{0:T(512)(128)(2,1)S(1)}, bf16[512]{0:T(512)(128)(2,1)}, u32[]{:S(2)}) copy-start(bf16[512]{0:T(512)(128)(2,1)} %param.19) | copy-start | bytes 3076
  6.5 8.3 %copy-start.24 = (bf16[512]{0:T(512)(128)(2,1)S(1)}, bf16[512]{0:T(512)(128)(2,1)}, u32[]{:S(2)}) copy-start(bf16[512]{0:T(512)(128)(2,1)} %param.20) | copy-start | bytes 3076
  6.6 71.5 %all-reduce.3.cloned.1.call-start = ((), (), s32[]{:S(2)}) async-start(), calls=%async_computation.5 | async-start | bytes 2621440 | tf_op jit(solution)/shard_map/psum | solution.py:90
  12.8 2.1 %copy-start.11 = (bf16[2,512,512]{2,1,0:T(8,128)(2,1)S(1)}, bf16[2,512,512]{2,1,0:T(8,128)(2,1)}, u32[]{:S(2)}) copy-start(bf16[2,512,512]{2,1,0:T(8,128)(2,1)} %param.22) | copy-start | bytes 3145732
  12.8 2.6 %copy-start.22 = (s32[8]{0:T(128)S(1)}, s32[8]{0:T(128)}, u32[]{:S(2)}) copy-start(s32[8]{0:T(128)} %param.26) | copy-start | bytes 100
  12.8 2.6 %copy-start.27 = (s32[8]{0:T(128)S(1)}, s32[8]{0:T(128)}, u32[]{:S(2)}) copy-start(s32[8]{0:T(128)} %param.27) | copy-start | bytes 100
  15.5 8.6 %copy-start.18 = (pred[64]{0:T(512)(128)(4,1)}, pred[64]{0:T(512)(128)(4,1)S(1)}, u32[]{:S(2)}) copy-start(pred[64]{0:T(512)(128)(4,1)S(1)} %get-tuple-element.32) | copy-start | bytes 196
  15.5 8.6 %copy-start.20 = (pred[64]{0:T(512)(128)(4,1)}, pred[64]{0:T(512)(128)(4,1)S(1)}, u32[]{:S(2)}) copy-start(pred[64]{0:T(512)(128)(4,1)S(1)} %get-tuple-element.33) | copy-start | bytes 196
  78.0 1.5 copy-start.14
  78.0 1.6 copy-start.15
  81.3 5.3 %copy-start.1 = (f32[4,64,8,512]{3,2,1,0:T(8,128)}, f32[4,64,8,512]{3,2,1,0:T(8,128)S(1)}, u32[]{:S(2)}) copy-start(f32[4,64,8,512]{3,2,1,0:T(8,128)S(1)} %get-tuple-element.37) | copy-start | bytes 12582916
  82.1 4.4 %copy-start.3 = (f32[4,64,8,512]{3,2,1,0:T(8,128)}, f32[4,64,8,512]{3,2,1,0:T(8,128)S(1)}, u32[]{:S(2)}) copy-start(f32[4,64,8,512]{3,2,1,0:T(8,128)S(1)} %get-tuple-element.35) | copy-start | bytes 12582916
  82.9 1.3 copy-start.6
  84.2 2.3 %copy-start.19 = (pred[64]{0:T(512)(128)(4,1)S(1)}, pred[64]{0:T(512)(128)(4,1)}, u32[]{:S(2)}) copy-start(pred[64]{0:T(512)(128)(4,1)} %copy-done.18) | copy-start | bytes 196
  84.2 2.4 %copy-start.21 = (pred[64]{0:T(512)(128)(4,1)S(1)}, pred[64]{0:T(512)(128)(4,1)}, u32[]{:S(2)}) copy-start(pred[64]{0:T(512)(128)(4,1)} %copy-done.20) | copy-start | bytes 196
  84.2 2.5 %copy-start.4 = (bf16[2,1024,4,128]{3,2,1,0:T(4,128)(2,1)S(1)}, bf16[2,1024,4,128]{3,2,1,0:T(4,128)(2,1)}, u32[]{:S(2)}) copy-start(bf16[2,1024,4,128]{3,2,1,0:T(4,128)(2,1)} %reshape.290) | copy-start | bytes 6291460
  86.6 1.7 copy-start.25
  86.6 1.7 copy-start.26
  88.4 1.5 copy-start.12
  91.5 15.7 %all-to-all-start.1 = ((f32[8,1,256]{2,1,0:T(1,128)}), f32[8,1,256]{2,1,0:T(1,128)S(1)}, u32[]{:S(2)}, u32[]{:S(2)}) async-start(f32[8,1,256]{2,1,0:T(1,128)} %reshape.303), calls=%async_computation.1 | async-start | bytes 16384 | tf_op jit(solution)/shard_map/all_to_all | solution.py:184
  94.9 3.6 %copy-start.2 = (f32[4,64,8,512]{3,2,1,0:T(8,128)S(1)}, f32[4,64,8,512]{3,2,1,0:T(8,128)}, u32[]{:S(2)}) copy-start(f32[4,64,8,512]{3,2,1,0:T(8,128)} %copy-done.1) | copy-start | bytes 12582916
  94.9 3.7 %copy-start.8 = (bf16[1,512,512]{1,2,0:T(8,128)(2,1)S(1)}, bf16[1,512,512]{1,2,0:T(8,128)(2,1)}, u32[]{:S(2)}) copy-start(bf16[1,512,512]{1,2,0:T(8,128)(2,1)} %copy.243) | copy-start | bytes 1572868
  100.2 1.0 copy-start.5
  101.2 4.7 %copy-start.7 = (f32[2,8,4,8,8]{3,4,1,2,0:T(8,128)S(1)}, f32[2,8,4,8,8]{3,4,1,2,0:T(8,128)}, u32[]{:S(2)}) copy-start(f32[2,8,4,8,8]{3,4,1,2,0:T(8,128)} %copy-done.6) | copy-start | bytes 49156
  102.6 3.4 %copy-start.16 = (f32[2,8,4,8]{3,1,2,0:T(8,128)S(1)}, f32[2,8,4,8]{3,1,2,0:T(8,128)}, u32[]{:S(2)}) copy-start(f32[2,8,4,8]{3,1,2,0:T(8,128)} %get-tuple-element.24) | copy-start | bytes 6148
  102.6 3.7 %copy-start.13 = (f32[1,64,4,8]{3,1,2,0:T(8,128)S(1)}, f32[1,64,4,8]{3,1,2,0:T(8,128)}, u32[]{:S(2)}) copy-start(f32[1,64,4,8]{3,1,2,0:T(8,128)} %copy-done.12) | copy-start | bytes 24580
  107.2 10.5 %all-to-all-start.2 = ((f32[8,1,256]{2,1,0:T(1,128)}), f32[8,1,256]{2,1,0:T(1,128)S(1)}, u32[]{:S(2)}, u32[]{:S(2)}) async-start(f32[8,1,256]{2,1,0:T(1,128)} %reshape.305), calls=%async_computation.2 | async-start | bytes 16384 | tf_op jit(solution)/shard_map/all_to_all | solution.py:185
  117.7 30.1 %all-to-all-start = ((f32[1,64,4,8,128]{4,3,2,0,1:T(8,128)}), f32[1,64,4,8,128]{4,3,2,0,1:T(8,128)S(1)}, u32[]{:S(2)}, u32[]{:S(2)}) async-start(f32[1,64,4,8,128]{4,3,2,0,1:T(8,128)} %copy.197), calls=%async_computation | async-start | bytes 2097152 | tf_op jit(solution)/shard_map/all_to_all | solution.py:186
  121.2 58.1 %reduce-scatter.2.cloned.1.call-start = ((), (), s32[]{:S(2)}) async-start(), calls=%async_computation.4 | async-start | bytes 393216 | tf_op jit(solution)/shard_map/reduce_scatter | solution.py:195
Sparse Core Ops, SparseCore 0:
  14.9 63.0 all-reduce.2
  169.0 10.2 reduce-scatter.1
where the time goes:
time: 188 us
  waiting for transfers between devices  86.1 us (46%)
  local copies, waits for them, and re-layouts  26 us (14%)
  matrix products  24.8 us (13%)
  blocking collectives  14.9 us (8%)
  between operations  14 us (7%)
  starting transfers between devices  11.9 us (6%)
  other arithmetic  9.87 us (5%)
    psum x1, waiting for transfers between devices, body(): q_sum, k_sum, v_sum = lax.psum((q_part, k_part, v_part), ('roll', 'seq'))  49.6 us
    all_to_all x1, waiting for transfers between devices, body(): lax.all_to_all(numer_all[None], ('roll', 'seq'), split_axis=1, concat_axi...  23.6 us
    all_gather x1, blocking collectives, body(): attention = lax.all_gather(share, ('roll', 'seq'), axis=0, tiled=True)  14.9 us
    reduce_scatter x1, waiting for transfers between devices, body(): lax.psum_scatter(jnp.dot(attention, w_out, preferred_element_type=jnp.flo...  10.4 us
    unnamed x66, local copies, waits for them, and re-layouts  8.2 us
    dot_general x1, matrix products, body(): q_part = jnp.dot(hidden, w_query, preferred_element_type=jnp.float32)  6.18 us
    dot_general x1, matrix products, body(): jnp.dot(attention, w_out, preferred_element_type=jnp.float32)  5.67 us
    all_to_all x1, starting transfers between devices, body(): lax.all_to_all(total_all[None], ('roll', 'seq'), split_axis=1, concat_axi...  4.86 us
  transfers between devices with their start and end apart: 5, of which 4 were waited for; matrix products, arithmetic and copies ran while one was open for 16% of the time, Pallas kernels for 0%

commit v1 on v0

v1 whole, which is shorter than its diff:
```python
import functools
import math

import jax
import jax.numpy as jnp
import numpy as np
from jax import lax
from jax.experimental import pallas as pl
from jax.experimental.pallas import tpu as pltpu
from jax.sharding import PartitionSpec as P

HD = 128
GUESS = 8
ROPE_BASE = 1000000.0
NEG_FILL = -1e30
SCALE = 1.0 / math.sqrt(HD)
MESH = pl.DeviceIdType.MESH
F32 = jnp.float32
BF16 = jnp.bfloat16


def dot(a, b):
    return jnp.dot(a, b, preferred_element_type=F32)


def dot_nt(a, b):
    return lax.dot_general(a, b, (((1,), (1,)), ((), ())), preferred_element_type=F32)


def kernel(
    dims,
    lens_ref,
    prompt_ref,
    freq_ref,
    bq_ref,
    bk_ref,
    bv_ref,
    hid_ref,
    wq_ref,
    wk_ref,
    wv_ref,
    wo_ref,
    pk_ref,
    pv_ref,
    sk_ref,
    sv_ref,
    out_ref,
    hid,
    wq,
    wk,
    wv,
    wo,
    kb,
    vb,
    skb,
    svb,
    vt,
    svt,
    sibout,
    sibin,
    zs,
    zin,
    qg,
    kn,
    vn,
    onum,
    ostat,
    nsend,
    nin,
    stsend,
    stin,
    att,
    acc,
    tin,
    ld,
    ldw,
    ldo,
    sw_s,
    sw_r,
    pr_s,
    pr_r,
    rs_s,
    rs_r,
    ag_s,
    ag_r,
    nu_s,
    nu_r,
    st_s,
    st_r,
    at_s,
    at_r,
    fw_s,
    fw_r,
    tp_s,
    tp_r,
):
    R, T = dims["R"], dims["T"]
    kvw, gq, rz, M = dims["kvw"], dims["gq"], dims["rz"], dims["M"]
    kvh, qhalf, pre, suf = dims["kvh"], dims["qhalf"], dims["pre"], dims["suf"]
    prompts, per = dims["prompts"], dims["per"]
    gw = gq * HD
    cw = gw + 2 * HD
    W = kvw * HD
    L = gq * rz
    mt = M // T
    z = lax.axis_index("roll")
    c = lax.axis_index("seq")
    t = lax.axis_index("tp")
    sib = 1 - c

    def kv_off(core):
        if kvh >= 2:
            return pl.multiple_of(core * W, HD)
        return 0

    def q_off(core, k):
        return pl.multiple_of((core * qhalf + k * gq) * HD, HD)

    halves = (sib, c)

    loads = [pltpu.make_async_copy(hid_ref, hid, ld.at[0])]
    loads[0].start()
    wload = {}
    for s in range(2):
        a = pltpu.make_async_copy(wk_ref.at[:, pl.ds(kv_off(halves[s]), W)], wk.at[s], ld.at[1 + s])
        b = pltpu.make_async_copy(wv_ref.at[:, pl.ds(kv_off(halves[s]), W)], wv.at[s], ld.at[3 + s])
        for k in range(kvw):
            wload[s, k] = pltpu.make_async_copy(
                wq_ref.at[:, pl.ds(q_off(halves[s], k), gw)], wq.at[s, k], ldw.at[s, k]
            )
            wload[s, k].start()
            if k == 0:
                a.start()
                b.start()
        loads += [a, b]

    barrier = pltpu.get_barrier_semaphore()
    for o in range(1, R):
        pl.semaphore_signal(
            barrier, inc=1, device_id={"roll": lax.rem(z + o, R)}, device_id_type=MESH
        )
    pl.semaphore_signal(barrier, inc=1, device_id={"seq": sib}, device_id_type=MESH)
    for o in range(1, T):
        pl.semaphore_signal(
            barrier, inc=1, device_id={"tp": lax.rem(t + o, T)}, device_id_type=MESH
        )
    pl.semaphore_wait(barrier, R + T - 1)

    def project(s, k):
        x = hid[...]
        cols = slice(k * HD, (k + 1) * HD)
        return dot(x, wq[s, k]), dot(x, wk[s, :, cols]), dot(x, wv[s, :, cols])

    pairs = []
    loads[0].wait()
    for k in range(kvw):
        wload[0, k].wait()
        if k == 0:
            loads[1].wait()
            loads[2].wait()
        a, b, d = project(0, k)
        sibout[k, :, 0:gw] = a
        sibout[k, :, gw : gw + HD] = b
        sibout[k, :, gw + HD : cw] = d
        cp = pltpu.make_async_remote_copy(
            sibout.at[k], sibin.at[k], pr_s.at[k], pr_r.at[k],
            device_id={"seq": sib}, device_id_type=MESH,
        )
        cp.start()
        pairs.append(cp)

    kv_local, kv_remote = [], []
    for i, (src, dst) in enumerate(((pk_ref, kb), (pv_ref, vb), (sk_ref, skb), (sv_ref, svb))):
        cp = pltpu.make_async_copy(
            src.at[:, :, pl.ds(kv_off(c), W)], dst.at[0], ld.at[5 + i]
        )
        cp.start()
        kv_local.append(cp)
        cp = pltpu.make_async_remote_copy(
            src.at[:, :, pl.ds(kv_off(sib), W)], dst.at[1], sw_s.at[i], sw_r.at[i],
            device_id={"seq": sib}, device_id_type=MESH,
        )
        cp.start()
        kv_remote.append(cp)
    oload = {}
    for s, half in ((0, c), (1, sib)):
        for k in range(kvw):
            oload[s, k] = pltpu.make_async_copy(
                wo_ref.at[pl.ds(q_off(half, k), gw)], wo.at[s, k], ldo.at[s, k]
            )
            oload[s, k].start()

    def along(src_of, dst_of, sems, semr, o):
        dest = lax.rem(z + o, R)
        return pltpu.make_async_remote_copy(
            src_of(dest), dst_of(z), sems, semr, device_id={"roll": dest}, device_id_type=MESH
        )

    def arrived(dst_of, sems, semr, o):
        source = lax.rem(z + R - o, R)
        ref = dst_of(source)
        pltpu.make_async_remote_copy(
            ref, ref, sems, semr, device_id={"roll": lax.rem(z + o, R)}, device_id_type=MESH
        ).wait_recv()
        return source

    sends = []

    for k in range(kvw):
        wload[1, k].wait()
        if k == 0:
            loads[3].wait()
            loads[4].wait()
        a, b, d = project(1, k)
        pairs[k].wait()
        zs[k, :, 0:gw] = a + sibin[k, :, 0:gw]
        zs[k, :, gw : gw + HD] = b + sibin[k, :, gw : gw + HD]
        zs[k, :, gw + HD : cw] = d + sibin[k, :, gw + HD : cw]
        for o in range(1, R):
            cp = along(
                lambda dest, k=k: zs.at[k, pl.ds(pl.multiple_of(dest * rz, rz), rz)],
                lambda me, k=k: zin.at[k, me],
                rs_s.at[k, o], rs_r.at[k, o], o,
            )
            cp.start()
            sends.append(cp)

    tok = lax.broadcasted_iota(jnp.int32, (rz, HD), 0)
    base = jnp.zeros((rz, HD), jnp.int32)
    for i in range(per):
        base = jnp.where(tok // GUESS == i, lens_ref[z * per + i], base)
    position = (dims["prefix_total"] + base + tok % GUESS).astype(F32)
    angles = position * freq_ref[...]
    cosine = jnp.cos(angles)
    lane = lax.broadcasted_iota(jnp.int32, (rz, HD), 1)
    sine = jnp.sin(angles)
    sine = jnp.where(lane < HD // 2, -sine, sine)

    def rotate(x):
        return x * cosine + pltpu.roll(x, HD // 2, 1) * sine

    for cp in kv_local:
        cp.wait()
    for cp in kv_remote:
        cp.wait()
    for k in range(kvw):
        cols = slice(k * HD, (k + 1) * HD)
        for s in range(2):
            for p in range(prompts):
                vt[k, p * HD : (p + 1) * HD, s * pre : (s + 1) * pre] = vb[s, p, :, cols].T
            for p in range(per):
                svt[k, p * HD : (p + 1) * HD, s * suf : (s + 1) * suf] = svb[s, p, :, cols].T

    for k in range(kvw):
        for o in range(1, R):
            arrived(lambda src, k=k: zin.at[k, src], rs_s.at[k, o], rs_r.at[k, o], o)
        x = zs[k, pl.ds(pl.multiple_of(z * rz, rz), rz), :]
        for o in range(1, R):
            x = x + zin[k, lax.rem(z + R - o, R)]
        xq = x[:, :gw] + bq_ref[:, pl.ds(q_off(c, k), gw)].astype(F32)
        kcol = pl.ds(pl.multiple_of(kv_off(c) + k * HD, HD), HD)
        for h in range(gq):
            qg[k, z, h] = rotate(xq[:, h * HD : (h + 1) * HD]).astype(BF16)
        for o in range(1, R):
            cp = along(
                lambda dest, k=k: qg.at[k, z], lambda me, k=k: qg.at[k, me],
                ag_s.at[k, o], ag_r.at[k, o], o,
            )
            cp.start()
            sends.append(cp)
        kn[k] = rotate(x[:, gw : gw + HD] + bk_ref[:, kcol].astype(F32))
        vn[k] = x[:, gw + HD :] + bv_ref[:, kcol].astype(F32)

    toks = lax.broadcasted_iota(jnp.int32, (rz, HD), 0)
    parts = [(toks // GUESS == i).astype(F32).astype(BF16) for i in range(per)]
    ltok = lax.broadcasted_iota(jnp.int32, (1, L), 1) % rz
    live = jnp.zeros((1, L), jnp.int32)
    for i in range(per):
        live = jnp.where(ltok // GUESS == i, lens_ref[z * per + i], live)
    for k in range(kvw):
        cols = slice(k * HD, (k + 1) * HD)
        q = qg[k, z]
        keys = jnp.concatenate(
            [jnp.concatenate([skb[s, p, :, cols] for p in range(per)], axis=1) for s in range(2)],
            axis=0,
        )
        qs = jnp.concatenate([(q * m[None]).reshape(L, HD) for m in parts], axis=1)
        s_suf = dot_nt(keys, qs)
        place = lax.broadcasted_iota(jnp.int32, (2 * suf, L), 0)
        place = (place + c * suf) % (2 * suf)
        s_suf = jnp.where(place < live, s_suf, NEG_FILL)
        s_new = dot_nt(kn[k].astype(BF16), q.reshape(L, HD))
        row = lax.broadcasted_iota(jnp.int32, (rz, L), 0)
        col = lax.broadcasted_iota(jnp.int32, (rz, L), 1) % rz
        seen = (row // GUESS == col // GUESS) & (row % GUESS <= col % GUESS)
        s_new = jnp.where(seen, s_new, NEG_FILL)
        peak = jnp.maximum(
            jnp.max(s_suf, axis=0, keepdims=True), jnp.max(s_new, axis=0, keepdims=True)
        )
        w_suf = jnp.exp((s_suf - peak) * SCALE)
        w_new = jnp.exp((s_new - peak) * SCALE)
        both = dot(svt[k], w_suf.astype(BF16))
        numer = dot(vn[k].T.astype(BF16), w_new.astype(BF16))
        for i in range(per):
            numer = numer + jnp.where(ltok // GUESS == i, both[i * HD : (i + 1) * HD], 0.0)
        onum[k] = numer
        ostat[k, 0:1, :] = peak
        ostat[k, 1:2, :] = jnp.sum(w_suf, axis=0, keepdims=True) + jnp.sum(
            w_new, axis=0, keepdims=True
        )

    zb = max(1, min(R, 256 // L))
    for k in range(kvw):
        cols = slice(k * HD, (k + 1) * HD)
        for o in range(1, R):
            arrived(lambda src, k=k: qg.at[k, src], ag_s.at[k, o], ag_r.at[k, o], o)
        keys = jnp.concatenate(
            [
                jnp.concatenate([kb[s, p, :, cols] for p in range(prompts)], axis=1)
                for s in range(2)
            ],
            axis=0,
        )
        for first in range(0, R, zb):
            blocks = []
            pick = jnp.zeros((1, zb * L), jnp.int32)
            wide = lax.broadcasted_iota(jnp.int32, (1, zb * L), 1)
            for j in range(zb):
                owner = jnp.zeros((rz, HD), jnp.int32)
                for i in range(per):
                    which = prompt_ref[(first + j) * per + i]
                    owner = jnp.where(toks // GUESS == i, which, owner)
                    here = (wide // L == j) & ((wide % rz) // GUESS == i)
                    pick = jnp.where(here, which, pick)
                q = qg[k, first + j]
                blocks.append(
                    jnp.concatenate(
                        [
                            (q * (owner == p).astype(F32).astype(BF16)[None]).reshape(L, HD)
                            for p in range(prompts)
                        ],
                        axis=1,
                    )
                )
            s_pre = dot_nt(keys, jnp.concatenate(blocks, axis=0))
            peak = jnp.max(s_pre, axis=0, keepdims=True)
            w_pre = jnp.exp((s_pre - peak) * SCALE)
            total = jnp.sum(w_pre, axis=0, keepdims=True)
            both = dot(vt[k], w_pre.astype(BF16))
            numer = jnp.zeros((HD, zb * L), F32)
            for p in range(prompts):
                numer = jnp.where(pick == p, both[p * HD : (p + 1) * HD], numer)
            numer = numer.astype(BF16)
            for j in range(zb):
                nsend[k, first + j] = numer[:, j * L : (j + 1) * L]
                stsend[k, first + j, 0:1, :] = peak[:, j * L : (j + 1) * L]
                stsend[k, first + j, 1:2, :] = total[:, j * L : (j + 1) * L]
        for o in range(1, R):
            cp = along(
                lambda dest, k=k: nsend.at[k, dest], lambda me, k=k: nin.at[k, me],
                nu_s.at[k, o], nu_r.at[k, o], o,
            )
            cp.start()
            sends.append(cp)
            cp = along(
                lambda dest, k=k: stsend.at[k, dest], lambda me, k=k: stin.at[k, me],
                st_s.at[k, o], st_r.at[k, o], o,
            )
            cp.start()
            sends.append(cp)

    forwards = []

    def forward(k, o, place):
        rows = pl.ds(pl.multiple_of(place * rz, rz), rz)
        cp = pltpu.make_async_remote_copy(
            att.at[0, k, rows], att.at[1, k, rows], fw_s.at[k, o], fw_r.at[k, o],
            device_id={"seq": sib}, device_id_type=MESH,
        )
        cp.start()
        forwards.append(cp)

    for k in range(kvw):
        for o in range(1, R):
            arrived(lambda src, k=k: nin.at[k, src], nu_s.at[k, o], nu_r.at[k, o], o)
            arrived(lambda src, k=k: stin.at[k, src], st_s.at[k, o], st_r.at[k, o], o)
        stats = [(ostat[k, 0:1, :], ostat[k, 1:2, :]), (stsend[k, z, 0:1, :], stsend[k, z, 1:2, :])]
        numers = [onum[k], nsend[k, z].astype(F32)]
        for o in range(1, R):
            source = lax.rem(z + R - o, R)
            stats.append((stin[k, source, 0:1, :], stin[k, source, 1:2, :]))
            numers.append(nin[k, source].astype(F32))
        top = functools.reduce(jnp.maximum, [peak for peak, _ in stats])
        total = jnp.zeros((1, L), F32)
        numer = jnp.zeros((HD, L), F32)
        for (peak, part), piece in zip(stats, numers):
            factor = jnp.exp((peak - top) * SCALE)
            total = total + part * factor
            numer = numer + piece * factor
        share = (numer / total).T.astype(BF16)
        mine = pl.ds(pl.multiple_of(z * rz, rz), rz)
        att[0, k, mine, :] = jnp.concatenate(
            [share[h * rz : (h + 1) * rz] for h in range(gq)], axis=1
        )
        for o in range(1, R):
            cp = along(
                lambda dest, k=k: att.at[0, k, mine],
                lambda me, k=k: att.at[0, k, pl.ds(pl.multiple_of(me * rz, rz), rz)],
                at_s.at[k, o], at_r.at[k, o], o,
            )
            cp.start()
            sends.append(cp)
        forward(k, 0, z)

    total = jnp.zeros(acc.shape, F32)
    for k in range(kvw):
        for o in range(1, R):
            source = arrived(
                lambda src, k=k: att.at[0, k, pl.ds(pl.multiple_of(src * rz, rz), rz)],
                at_s.at[k, o], at_r.at[k, o], o,
            )
            forward(k, o, source)
        oload[0, k].wait()
        total = total + dot(att[0, k], wo[0, k])
    for cp in forwards:
        cp.wait()
    for k in range(kvw):
        oload[1, k].wait()
        total = total + dot(att[1, k], wo[1, k])
    acc[...] = total

    tps = []
    for o in range(1, T):
        dest = lax.rem(t + o, T)
        cp = pltpu.make_async_remote_copy(
            acc.at[pl.ds(pl.multiple_of(dest * mt, mt), mt)], tin.at[o - 1],
            tp_s.at[o], tp_r.at[o], device_id={"tp": dest}, device_id_type=MESH,
        )
        cp.start()
        tps.append(cp)
    result = acc[pl.ds(pl.multiple_of(t * mt, mt), mt), :]
    for o in range(1, T):
        tps[o - 1].wait()
        result = result + tin[o - 1]
    out_ref[...] = result.astype(BF16)
    for cp in sends:
        cp.wait_send()


def body(
    sizes,
    hidden,
    w_query,
    w_key,
    w_value,
    b_query,
    b_key,
    b_value,
    w_out,
    prefix_keys,
    prefix_values,
    suffix_keys,
    suffix_values,
    suffix_lengths,
    prompt_of,
):
    R, S, T = sizes
    M, K = hidden.shape
    q_heads, kvh = w_query.shape[1] // HD, w_key.shape[1] // HD
    prompts, pre, _ = prefix_keys.shape
    per, suf, _ = suffix_keys.shape
    N = w_out.shape[1]
    qhalf = q_heads // S
    kvw = max(kvh // S, 1)
    gq = qhalf // kvw
    rz = per * GUESS
    dims = dict(
        R=R, T=T, M=M, kvw=kvw, gq=gq, rz=rz, kvh=kvh, qhalf=qhalf, pre=pre, suf=suf,
        prompts=prompts, per=per, prefix_total=pre * R * S,
    )
    W, gw, L = kvw * HD, gq * HD, gq * rz
    cw = gw + 2 * HD
    steps = np.arange(HD // 2).astype(np.float32) * np.float32(2.0 / HD)
    freqs = np.exp(np.float32(-math.log(ROPE_BASE)) * steps).astype(np.float32)
    freqs = jnp.asarray(np.concatenate([freqs, freqs])[None])
    smem = pl.BlockSpec(memory_space=pltpu.SMEM)
    vmem = pl.BlockSpec(memory_space=pltpu.VMEM)
    hbm = pl.BlockSpec(memory_space=pl.ANY)
    dma = pltpu.SemaphoreType.DMA
    return pl.pallas_call(
        functools.partial(kernel, dims),
        out_shape=jax.ShapeDtypeStruct((M // T, N), BF16),
        in_specs=[smem, smem] + [vmem] * 4 + [hbm] * 9,
        out_specs=vmem,
        scratch_shapes=[
            pltpu.VMEM((M, K), BF16),
            pltpu.VMEM((S, kvw, K, gw), BF16),
            pltpu.VMEM((S, K, W), BF16),
            pltpu.VMEM((S, K, W), BF16),
            pltpu.VMEM((S, kvw, gw, N), BF16),
            pltpu.VMEM((S, prompts, pre, W), BF16),
            pltpu.VMEM((S, prompts, pre, W), BF16),
            pltpu.VMEM((S, per, suf, W), BF16),
            pltpu.VMEM((S, per, suf, W), BF16),
            pltpu.VMEM((kvw, prompts * HD, S * pre), BF16),
            pltpu.VMEM((kvw, per * HD, S * suf), BF16),
            pltpu.VMEM((kvw, M, cw), F32),
            pltpu.VMEM((kvw, M, cw), F32),
            pltpu.VMEM((kvw, M, cw), F32),
            pltpu.VMEM((kvw, R, rz, cw), F32),
            pltpu.VMEM((kvw, R, gq, rz, HD), BF16),
            pltpu.VMEM((kvw, rz, HD), F32),
            pltpu.VMEM((kvw, rz, HD), F32),
            pltpu.VMEM((kvw, HD, L), F32),
            pltpu.VMEM((kvw, 8, L), F32),
            pltpu.VMEM((kvw, R, HD, L), BF16),
            pltpu.VMEM((kvw, R, HD, L), BF16),
            pltpu.VMEM((kvw, R, 8, L), F32),
            pltpu.VMEM((kvw, R, 8, L), F32),
            pltpu.VMEM((S, kvw, M, gw), BF16),
            pltpu.VMEM((M, N), F32),
            pltpu.VMEM((max(T - 1, 1), M // T, N), F32),
            dma((9,)),
            dma((S, kvw)),
            dma((S, kvw)),
            dma((4,)),
            dma((4,)),
            dma((kvw,)),
            dma((kvw,)),
        ]
        + [dma((kvw, R))] * 12
        + [dma((T,))] * 2,
        compiler_params=pltpu.CompilerParams(
            collective_id=0, has_side_effects=True, vmem_limit_bytes=60 * 1024 * 1024
        ),
        cost_estimate=pl.CostEstimate(
            flops=2 * M * K * (w_query.shape[1] + 2 * w_key.shape[1]) + 2 * M * N * w_out.shape[0],
            bytes_accessed=2 * (w_query.size + 2 * w_key.size + w_out.size)
            + 4 * (prefix_keys.size + suffix_keys.size),
            transcendentals=0,
        ),
    )(
        suffix_lengths,
        prompt_of,
        freqs,
        b_query[None],
        b_key[None],
        b_value[None],
        hidden,
        w_query,
        w_key,
        w_value,
        w_out,
        prefix_keys,
        prefix_values,
        suffix_keys,
        suffix_values,
    )


def solution(mesh):
    sizes = (mesh.shape["roll"], mesh.shape["seq"], mesh.shape["tp"])
    return jax.shard_map(
        functools.partial(body, sizes),
        mesh=mesh,
        in_specs=(
            P("groups", ("roll", "seq")),
            P(("roll", "seq"), "tp"),
            P(("roll", "seq"), "tp"),
            P(("roll", "seq"), "tp"),
            P("tp"),
            P("tp"),
            P("tp"),
            P("tp", ("roll", "seq")),
            P("groups", ("roll", "seq"), "tp"),
            P("groups", ("roll", "seq"), "tp"),
            P(("groups", "roll"), "seq", "tp"),
            P(("groups", "roll"), "seq", "tp"),
            P("groups"),
            P("groups"),
        ),
        out_specs=P(("groups", "tp"), ("roll", "seq")),
        check_vma=False,
    )
```

time: 188 us -> 58.9 us (0.31)
  waiting for transfers between devices: 86.1 us -> 0 us
  Pallas kernels: 0 us -> 53.3 us
  matrix products: 24.8 us -> 0 us
  local copies, waits for them, and re-layouts: 26 us -> 5.28 us
  blocking collectives: 14.9 us -> 0 us
  between operations: 14 us -> 0.01 us
  starting transfers between devices: 11.9 us -> 0 us
  other arithmetic: 9.87 us -> 0 us
    pallas_call x0 -> x1, Pallas kernels: none -> 53.3 us  [body(): pl.pallas_call(functools.partial(kernel, dims), out_shape=jax.ShapeDtypeS...]
    psum x1 -> x0, waiting for transfers between devices: 49.6 us -> none  [body(): q_sum, k_sum, v_sum = lax.psum((q_part, k_part, v_part), ('roll', 'seq'))]
    all_to_all x3 -> x0, waiting for transfers between devices: 26.1 us -> none  [the longest x1 23.6 us: body(): lax.all_to_all(numer_all[None], ('roll', 'seq'), split_axis=1, concat_axi...]
    dot_general x12 -> x0, matrix products: 24.8 us -> none  [the longest x1 6.18 us: body(): q_part = jnp.dot(hidden, w_query, preferred_element_type=jnp.float32)]
    all_gather x1 -> x0, blocking collectives: 14.9 us -> none  [body(): attention = lax.all_gather(share, ('roll', 'seq'), axis=0, tiled=True)]
    all_to_all x3 -> x0, starting transfers between devices: 11.9 us -> none  [the longest x1 4.86 us: body(): lax.all_to_all(total_all[None], ('roll', 'seq'), split_axis=1, concat_axi...]
    reduce_scatter x1 -> x0, waiting for transfers between devices: 10.4 us -> none  [body(): lax.psum_scatter(jnp.dot(attention, w_out, preferred_element_type=jnp.flo...]
    reshape x3 -> x0, local copies, waits for them, and re-layouts: 8.04 us -> none  [the longest x1 4 us: body(): suf_values = suffix_values.reshape(per_device, suf_dev, kv_heads, HD)]
  transfers between devices with their start and end apart: 5 -> 0, of which waited for: 4 -> 0; matrix products, arithmetic and copies ran while one was open for 16% -> 0% of each run, Pallas kernels for 0% -> 0%
where the time goes in v1:
time: 58.9 us; the launch traced here: 58.6 us
  Pallas kernels  53.3 us (90%)
  local copies, waits for them, and re-layouts  5.28 us (9%)
    pallas_call x1, Pallas kernels, body(): pl.pallas_call(functools.partial(kernel, dims), out_shape=jax.ShapeDtypeS...  53.3 us
    unnamed x1, local copies, waits for them, and re-layouts  1.47 us
    broadcast_in_dim x1, local copies, waits for them, and re-layouts, body(): b_query[None]  1.31 us
    broadcast_in_dim x1, local copies, waits for them, and re-layouts, body(): b_value[None]  1.26 us
    broadcast_in_dim x1, local copies, waits for them, and re-layouts, body(): b_key[None]  1.24 us

profile of v1, /device:TPU:0, one launch (start us, length us, event | category | flops | bytes accessed | tf_op | source)
XLA Modules:
  0.0 58.6 jit_solution(13276474572755882389)
XLA Ops:
  0.0 1.2 %broadcast_in_dim.10.bk_ref = bf16[1,512]{1,0:T(2,128)(2,1)} reshape(bf16[512]{0:T(512)(128)(2,1)} %param.20) | data formatting | bytes 2048 | tf_op jit(solution)/shard_map/broadcast_in_dim | solution.py:547
  1.2 1.3 %broadcast_in_dim.11.bv_ref = bf16[1,512]{1,0:T(2,128)(2,1)} reshape(bf16[512]{0:T(512)(128)(2,1)} %param.21) | data formatting | bytes 2048 | tf_op jit(solution)/shard_map/broadcast_in_dim | solution.py:548
  2.5 1.3 %broadcast_in_dim.9.bq_ref = bf16[1,4096]{1,0:T(2,128)(2,1)} reshape(bf16[4096]{0:T(1024)(128)(2,1)} %param.19) | data formatting | bytes 16384 | tf_op jit(solution)/shard_map/broadcast_in_dim | solution.py:546
  3.8 53.3 %shard_map.145 = bf16[32,1024]{1,0:T(8,128)(2,1)} custom-call(s32[8]{0:T(128)} %lens_ref.1, s32[8]{0:T(128)} %prompt_ref.1, f32[1,128]{1,0:T(1,128)} %constant.2.clone.freq_ref, bf16[1,4096]{1,0:T(2,128)(2,1)} %broadcast_in_dim.9.bq_ref, bf16[1,512]{1,0:T(2,128)(2,1)} %broadcast_in_dim.10.bk_ref, bf16[1,512]{1,0:T(2,128)(2,1)} %broadcast_in_dim.11.bv_ref, ...), custom_call_target="tpu_custom_call" | custom-call | flops 1207959552 | bytes 25165824 | tf_op jit(solution)/shard_map/pallas_call | solution.py:490
  57.1 1.5 %copy.17 = bf16[32,1024]{1,0:T(8,128)(2,1)} copy(bf16[32,1024]{1,0:T(8,128)(2,1)} %shard_map.145) | data formatting | bytes 131072

commit v2 on v1

--- a/solution.py
+++ b/solution.py
@@ -59,6 +59,7 @@
     sibout,
     sibin,
     zs,
+    zq,
     zin,
     qg,
     kn,
@@ -72,6 +73,9 @@
     att,
     acc,
     tin,
+    bq,
+    bk,
+    bv,
     ld,
     ldw,
     ldo,
@@ -117,22 +121,23 @@
         return pl.multiple_of((core * qhalf + k * gq) * HD, HD)
 
     halves = (sib, c)
+    hk = gq + 2
+    biases = ((bq_ref, bq), (bk_ref, bk), (bv_ref, bv))
 
     loads = [pltpu.make_async_copy(hid_ref, hid, ld.at[0])]
     loads[0].start()
     wload = {}
-    for s in range(2):
-        a = pltpu.make_async_copy(wk_ref.at[:, pl.ds(kv_off(halves[s]), W)], wk.at[s], ld.at[1 + s])
-        b = pltpu.make_async_copy(wv_ref.at[:, pl.ds(kv_off(halves[s]), W)], wv.at[s], ld.at[3 + s])
-        for k in range(kvw):
-            wload[s, k] = pltpu.make_async_copy(
-                wq_ref.at[:, pl.ds(q_off(halves[s], k), gw)], wq.at[s, k], ldw.at[s, k]
-            )
+    for k in range(kvw):
+        for s in range(2):
+            cols = pl.ds(q_off(halves[s], k), gw)
+            wload[s, k] = pltpu.make_async_copy(wq_ref.at[:, cols], wq.at[s, k], ldw.at[s, k])
             wload[s, k].start()
             if k == 0:
-                a.start()
-                b.start()
-        loads += [a, b]
+                cols = pl.ds(kv_off(halves[s]), W)
+                for src, dst, i in ((wk_ref, wk, 1), (wv_ref, wv, 3)):
+                    cp = pltpu.make_async_copy(src.at[:, cols], dst.at[s], ld.at[i + s])
+                    cp.start()
+                    loads.append(cp)
 
     barrier = pltpu.get_barrier_semaphore()
     for o in range(1, R):
@@ -151,9 +156,7 @@
         cols = slice(k * HD, (k + 1) * HD)
         return dot(x, wq[s, k]), dot(x, wk[s, :, cols]), dot(x, wv[s, :, cols])
 
-    pairs = []
-    loads[0].wait()
-    for k in range(kvw):
+    def other_half(k):
         wload[0, k].wait()
         if k == 0:
             loads[1].wait()
@@ -167,7 +170,23 @@
             device_id={"seq": sib}, device_id_type=MESH,
         )
         cp.start()
-        pairs.append(cp)
+        return cp
+
+    def own_half(k):
+        wload[1, k].wait()
+        if k == 0:
+            loads[3].wait()
+            loads[4].wait()
+        a, b, d = project(1, k)
+        zs[k, :, 0:gw] = a
+        zs[k, :, gw : gw + HD] = b
+        zs[k, :, gw + HD : cw] = d
+
+    loads[0].wait()
+    pairs = [other_half(0)]
+    own_half(0)
+    for k in range(1, kvw):
+        pairs.append(other_half(k))
 
     kv_local, kv_remote = [], []
     for i, (src, dst) in enumerate(((pk_ref, kb), (pv_ref, vb), (sk_ref, skb), (sv_ref, svb))):
@@ -206,24 +225,32 @@
 
     sends = []
 
-    for k in range(kvw):
-        wload[1, k].wait()
-        if k == 0:
-            loads[3].wait()
-            loads[4].wait()
-        a, b, d = project(1, k)
+    wlane = lax.broadcasted_iota(jnp.int32, (M, HD), 1)
+    for k in range(kvw):
+        if k > 0:
+            own_half(k)
         pairs[k].wait()
-        zs[k, :, 0:gw] = a + sibin[k, :, 0:gw]
-        zs[k, :, gw : gw + HD] = b + sibin[k, :, gw : gw + HD]
-        zs[k, :, gw + HD : cw] = d + sibin[k, :, gw + HD : cw]
+        powers = jnp.zeros((M, HD), F32)
+        for h in range(hk):
+            cols = slice(h * HD, (h + 1) * HD)
+            x = zs[k, :, cols] + sibin[k, :, cols]
+            zs[k, :, cols] = x
+            largest = jnp.maximum(jnp.max(jnp.abs(x), axis=1, keepdims=True), 1e-30)
+            power = jnp.ceil(jnp.log2(largest) + 0.01)
+            code = jnp.round(x * (32767.0 / jnp.exp2(power)))
+            zq[k, :, cols] = code.astype(jnp.int32).astype(jnp.int16)
+            powers = jnp.where(wlane == h, power, powers)
+        zq[k, :, cw : cw + HD] = powers.astype(jnp.int32).astype(jnp.int16)
         for o in range(1, R):
             cp = along(
-                lambda dest, k=k: zs.at[k, pl.ds(pl.multiple_of(dest * rz, rz), rz)],
+                lambda dest, k=k: zq.at[k, pl.ds(pl.multiple_of(dest * rz, rz), rz)],
                 lambda me, k=k: zin.at[k, me],
                 rs_s.at[k, o], rs_r.at[k, o], o,
             )
             cp.start()
             sends.append(cp)
+    for src, dst in biases:
+        dst[...] = src[...].astype(F32).reshape(dst.shape)
 
     tok = lax.broadcasted_iota(jnp.int32, (rz, HD), 0)
     base = jnp.zeros((rz, HD), jnp.int32)
@@ -239,25 +266,30 @@
     def rotate(x):
         return x * cosine + pltpu.roll(x, HD // 2, 1) * sine
 
-    for cp in kv_local:
-        cp.wait()
-    for cp in kv_remote:
-        cp.wait()
-    for k in range(kvw):
-        cols = slice(k * HD, (k + 1) * HD)
-        for s in range(2):
+    def turn(s):
+        for k in range(kvw):
+            cols = slice(k * HD, (k + 1) * HD)
             for p in range(prompts):
                 vt[k, p * HD : (p + 1) * HD, s * pre : (s + 1) * pre] = vb[s, p, :, cols].T
             for p in range(per):
                 svt[k, p * HD : (p + 1) * HD, s * suf : (s + 1) * suf] = svb[s, p, :, cols].T
 
+    for cp in kv_local:
+        cp.wait()
+    turn(0)
+
     for k in range(kvw):
         for o in range(1, R):
             arrived(lambda src, k=k: zin.at[k, src], rs_s.at[k, o], rs_r.at[k, o], o)
         x = zs[k, pl.ds(pl.multiple_of(z * rz, rz), rz), :]
-        for o in range(1, R):
-            x = x + zin[k, lax.rem(z + R - o, R)]
-        xq = x[:, :gw] + bq_ref[:, pl.ds(q_off(c, k), gw)].astype(F32)
+        sums = [x[:, h * HD : (h + 1) * HD] for h in range(hk)]
+        for o in range(1, R):
+            got = zin[k, lax.rem(z + R - o, R)].astype(jnp.int32).astype(F32)
+            units = jnp.exp2(got[:, cw:]) * (1.0 / 32767.0)
+            for h in range(hk):
+                sums[h] = sums[h] + got[:, h * HD : (h + 1) * HD] * units[:, h : h + 1]
+        x = jnp.concatenate(sums, axis=1)
+        xq = x[:, :gw] + bq[:, pl.ds(q_off(c, k), gw)]
         kcol = pl.ds(pl.multiple_of(kv_off(c) + k * HD, HD), HD)
         for h in range(gq):
             qg[k, z, h] = rotate(xq[:, h * HD : (h + 1) * HD]).astype(BF16)
@@ -268,8 +300,12 @@
             )
             cp.start()
             sends.append(cp)
-        kn[k] = rotate(x[:, gw : gw + HD] + bk_ref[:, kcol].astype(F32))
-        vn[k] = x[:, gw + HD :] + bv_ref[:, kcol].astype(F32)
+        kn[k] = rotate(x[:, gw : gw + HD] + bk[:, kcol])
+        vn[k] = x[:, gw + HD :] + bv[:, kcol]
+
+    for cp in kv_remote:
+        cp.wait()
+    turn(1)
 
     toks = lax.broadcasted_iota(jnp.int32, (rz, HD), 0)
     parts = [(toks // GUESS == i).astype(F32).astype(BF16) for i in range(per)]
@@ -312,8 +348,6 @@
     zb = max(1, min(R, 256 // L))
     for k in range(kvw):
         cols = slice(k * HD, (k + 1) * HD)
-        for o in range(1, R):
-            arrived(lambda src, k=k: qg.at[k, src], ag_s.at[k, o], ag_r.at[k, o], o)
         keys = jnp.concatenate(
             [
                 jnp.concatenate([kb[s, p, :, cols] for p in range(prompts)], axis=1)
@@ -323,16 +357,24 @@
         )
         for first in range(0, R, zb):
             blocks = []
+            places = []
+            for o in range(first, first + zb):
+                if o == 0:
+                    places.append(z)
+                else:
+                    places.append(
+                        arrived(lambda src, k=k: qg.at[k, src], ag_s.at[k, o], ag_r.at[k, o], o)
+                    )
             pick = jnp.zeros((1, zb * L), jnp.int32)
             wide = lax.broadcasted_iota(jnp.int32, (1, zb * L), 1)
             for j in range(zb):
                 owner = jnp.zeros((rz, HD), jnp.int32)
                 for i in range(per):
-                    which = prompt_ref[(first + j) * per + i]
+                    which = prompt_ref[places[j] * per + i]
                     owner = jnp.where(toks // GUESS == i, which, owner)
                     here = (wide // L == j) & ((wide % rz) // GUESS == i)
                     pick = jnp.where(here, which, pick)
-                q = qg[k, first + j]
+                q = qg[k, places[j]]
                 blocks.append(
                     jnp.concatenate(
                         [
@@ -352,22 +394,24 @@
                 numer = jnp.where(pick == p, both[p * HD : (p + 1) * HD], numer)
             numer = numer.astype(BF16)
             for j in range(zb):
-                nsend[k, first + j] = numer[:, j * L : (j + 1) * L]
-                stsend[k, first + j, 0:1, :] = peak[:, j * L : (j + 1) * L]
-                stsend[k, first + j, 1:2, :] = total[:, j * L : (j + 1) * L]
-        for o in range(1, R):
-            cp = along(
-                lambda dest, k=k: nsend.at[k, dest], lambda me, k=k: nin.at[k, me],
-                nu_s.at[k, o], nu_r.at[k, o], o,
-            )
-            cp.start()
-            sends.append(cp)
-            cp = along(
-                lambda dest, k=k: stsend.at[k, dest], lambda me, k=k: stin.at[k, me],
-                st_s.at[k, o], st_r.at[k, o], o,
-            )
-            cp.start()
-            sends.append(cp)
+                nsend[k, places[j]] = numer[:, j * L : (j + 1) * L]
+                stsend[k, places[j], 0:1, :] = peak[:, j * L : (j + 1) * L]
+                stsend[k, places[j], 1:2, :] = total[:, j * L : (j + 1) * L]
+                o = R - first - j
+                if o == R:
+                    continue
+                cp = along(
+                    lambda dest, k=k: nsend.at[k, dest], lambda me, k=k: nin.at[k, me],
+                    nu_s.at[k, o], nu_r.at[k, o], o,
+                )
+                cp.start()
+                sends.append(cp)
+                cp = along(
+                    lambda dest, k=k: stsend.at[k, dest], lambda me, k=k: stin.at[k, me],
+                    st_s.at[k, o], st_r.at[k, o], o,
+                )
+                cp.start()
+                sends.append(cp)
 
     forwards = []
 
@@ -412,7 +456,7 @@
             sends.append(cp)
         forward(k, 0, z)
 
-    total = jnp.zeros(acc.shape, F32)
+    total = jnp.zeros((M, dims["nb"] * acc.shape[2]), F32)
     for k in range(kvw):
         for o in range(1, R):
             source = arrived(
@@ -426,23 +470,27 @@
         cp.wait()
     for k in range(kvw):
         oload[1, k].wait()
-        total = total + dot(att[1, k], wo[1, k])
-    acc[...] = total
-
-    tps = []
-    for o in range(1, T):
-        dest = lax.rem(t + o, T)
-        cp = pltpu.make_async_remote_copy(
-            acc.at[pl.ds(pl.multiple_of(dest * mt, mt), mt)], tin.at[o - 1],
-            tp_s.at[o], tp_r.at[o], device_id={"tp": dest}, device_id_type=MESH,
-        )
-        cp.start()
-        tps.append(cp)
-    result = acc[pl.ds(pl.multiple_of(t * mt, mt), mt), :]
-    for o in range(1, T):
-        tps[o - 1].wait()
-        result = result + tin[o - 1]
-    out_ref[...] = result.astype(BF16)
+    nb, nc = dims["nb"], acc.shape[2]
+    tps = {}
+    for n in range(nb):
+        cols = slice(n * nc, (n + 1) * nc)
+        piece = total[:, cols]
+        for k in range(kvw):
+            piece = piece + dot(att[1, k], wo[1, k, :, cols])
+        acc[n] = piece
+        for o in range(1, T):
+            dest = lax.rem(t + o, T)
+            tps[n, o] = pltpu.make_async_remote_copy(
+                acc.at[n, pl.ds(pl.multiple_of(dest * mt, mt), mt)], tin.at[n, o - 1],
+                tp_s.at[n, o], tp_r.at[n, o], device_id={"tp": dest}, device_id_type=MESH,
+            )
+            tps[n, o].start()
+    for n in range(nb):
+        result = acc[n, pl.ds(pl.multiple_of(t * mt, mt), mt), :]
+        for o in range(1, T):
+            tps[n, o].wait()
+            result = result + tin[n, o - 1]
+        out_ref[:, n * nc : (n + 1) * nc] = result.astype(BF16)
     for cp in sends:
         cp.wait_send()
 
@@ -474,9 +522,10 @@
     kvw = max(kvh // S, 1)
     gq = qhalf // kvw
     rz = per * GUESS
+    nb = 2 if N % (2 * HD) == 0 else 1
     dims = dict(
         R=R, T=T, M=M, kvw=kvw, gq=gq, rz=rz, kvh=kvh, qhalf=qhalf, pre=pre, suf=suf,
-        prompts=prompts, per=per, prefix_total=pre * R * S,
+        prompts=prompts, per=per, prefix_total=pre * R * S, nb=nb,
     )
     W, gw, L = kvw * HD, gq * HD, gq * rz
     cw = gw + 2 * HD
@@ -507,7 +556,8 @@
             pltpu.VMEM((kvw, M, cw), F32),
             pltpu.VMEM((kvw, M, cw), F32),
             pltpu.VMEM((kvw, M, cw), F32),
-            pltpu.VMEM((kvw, R, rz, cw), F32),
+            pltpu.VMEM((kvw, M, cw + HD), jnp.int16),
+            pltpu.VMEM((kvw, R, rz, cw + HD), jnp.int16),
             pltpu.VMEM((kvw, R, gq, rz, HD), BF16),
             pltpu.VMEM((kvw, rz, HD), F32),
             pltpu.VMEM((kvw, rz, HD), F32),
@@ -518,8 +568,11 @@
             pltpu.VMEM((kvw, R, 8, L), F32),
             pltpu.VMEM((kvw, R, 8, L), F32),
             pltpu.VMEM((S, kvw, M, gw), BF16),
-            pltpu.VMEM((M, N), F32),
-            pltpu.VMEM((max(T - 1, 1), M // T, N), F32),
+            pltpu.VMEM((nb, M, N // nb), F32),
+            pltpu.VMEM((nb, max(T - 1, 1), M // T, N // nb), F32),
+            pltpu.VMEM((1, q_heads * HD), F32),
+            pltpu.VMEM((1, kvh * HD), F32),
+            pltpu.VMEM((1, kvh * HD), F32),
             dma((9,)),
             dma((S, kvw)),
             dma((S, kvw)),
@@ -529,7 +582,7 @@
             dma((kvw,)),
         ]
         + [dma((kvw, R))] * 12
-        + [dma((T,))] * 2,
+        + [dma((nb, T))] * 2,
         compiler_params=pltpu.CompilerParams(
             collective_id=0, has_side_effects=True, vmem_limit_bytes=60 * 1024 * 1024
         ),
@@ -543,9 +596,9 @@
         suffix_lengths,
         prompt_of,
         freqs,
-        b_query[None],
-        b_key[None],
-        b_value[None],
+        b_query,
+        b_key,
+        b_value,
         hidden,
         w_query,
         w_key,

time: 58.9 us -> 47.1 us (0.80)
  Pallas kernels: 53.3 us -> 45.4 us
  local copies, waits for them, and re-layouts: 5.28 us -> 1.47 us
    pallas_call x1, Pallas kernels: 53.3 us -> 45.4 us  [body(): pl.pallas_call(functools.partial(kernel, dims), out_shape=jax.ShapeDtypeS...]
    broadcast_in_dim x3 -> x0, local copies, waits for them, and re-layouts: 3.81 us -> none  [the longest x1 1.31 us: body(): b_query[None]]
where the time goes in v2:
time: 47.1 us; the launch traced here: 46.9 us
  Pallas kernels  45.4 us (96%)
  local copies, waits for them, and re-layouts  1.47 us (3%)
    pallas_call x1, Pallas kernels, body(): pl.pallas_call(functools.partial(kernel, dims), out_shape=jax.ShapeDtypeS...  45.4 us
    unnamed x1, local copies, waits for them, and re-layouts  1.47 us

profile of v2, /device:TPU:0, one launch (start us, length us, event | category | flops | bytes accessed | tf_op | source)
XLA Modules:
  0.0 46.9 jit_solution(5752150432794010396)
XLA Ops:
  0.0 45.4 %shard_map.145 = bf16[32,1024]{1,0:T(8,128)(2,1)} custom-call(s32[8]{0:T(128)} %lens_ref.1, s32[8]{0:T(128)} %prompt_ref.1, f32[1,128]{1,0:T(1,128)} %constant.2.clone.freq_ref, bf16[4096]{0:T(1024)(128)(2,1)} %bq_ref.1, bf16[512]{0:T(512)(128)(2,1)} %bk_ref.1, bf16[512]{0:T(512)(128)(2,1)} %bv_ref.1, bf16[64,1024]{1,0:T(8,128)(2,1)} %hid_ref.1, ...), custom_call_target="tpu_custom_call" | custom-call | flops 1207959552 | bytes 25165824 | tf_op jit(solution)/shard_map/pallas_call | solution.py:539
  45.4 1.5 %copy.17 = bf16[32,1024]{1,0:T(8,128)(2,1)} copy(bf16[32,1024]{1,0:T(8,128)(2,1)} %shard_map.145) | data formatting | bytes 131072

commit v3 on v2

--- a/solution.py
+++ b/solution.py
@@ -13,7 +13,7 @@
 GUESS = 8
 ROPE_BASE = 1000000.0
 NEG_FILL = -1e30
-SCALE = 1.0 / math.sqrt(HD)
+SCALE = math.log2(math.e) / math.sqrt(HD)
 MESH = pl.DeviceIdType.MESH
 F32 = jnp.float32
 BF16 = jnp.bfloat16
@@ -278,7 +278,7 @@
         cp.wait()
     turn(0)
 
-    for k in range(kvw):
+    def finish(k):
         for o in range(1, R):
             arrived(lambda src, k=k: zin.at[k, src], rs_s.at[k, o], rs_r.at[k, o], o)
         x = zs[k, pl.ds(pl.multiple_of(z * rz, rz), rz), :]
@@ -303,17 +303,14 @@
         kn[k] = rotate(x[:, gw : gw + HD] + bk[:, kcol])
         vn[k] = x[:, gw + HD :] + bv[:, kcol]
 
-    for cp in kv_remote:
-        cp.wait()
-    turn(1)
-
     toks = lax.broadcasted_iota(jnp.int32, (rz, HD), 0)
     parts = [(toks // GUESS == i).astype(F32).astype(BF16) for i in range(per)]
     ltok = lax.broadcasted_iota(jnp.int32, (1, L), 1) % rz
     live = jnp.zeros((1, L), jnp.int32)
     for i in range(per):
         live = jnp.where(ltok // GUESS == i, lens_ref[z * per + i], live)
-    for k in range(kvw):
+
+    def own_rows(k):
         cols = slice(k * HD, (k + 1) * HD)
         q = qg[k, z]
         keys = jnp.concatenate(
@@ -322,9 +319,14 @@
         )
         qs = jnp.concatenate([(q * m[None]).reshape(L, HD) for m in parts], axis=1)
         s_suf = dot_nt(keys, qs)
-        place = lax.broadcasted_iota(jnp.int32, (2 * suf, L), 0)
-        place = (place + c * suf) % (2 * suf)
-        s_suf = jnp.where(place < live, s_suf, NEG_FILL)
+        place = lax.broadcasted_iota(jnp.int32, (suf, L), 0)
+        s_suf = jnp.concatenate(
+            [
+                jnp.where(place < live - half * suf, s_suf[s * suf : (s + 1) * suf], NEG_FILL)
+                for s, half in ((0, c), (1, sib))
+            ],
+            axis=0,
+        )
         s_new = dot_nt(kn[k].astype(BF16), q.reshape(L, HD))
         row = lax.broadcasted_iota(jnp.int32, (rz, L), 0)
         col = lax.broadcasted_iota(jnp.int32, (rz, L), 1) % rz
@@ -333,8 +335,8 @@
         peak = jnp.maximum(
             jnp.max(s_suf, axis=0, keepdims=True), jnp.max(s_new, axis=0, keepdims=True)
         )
-        w_suf = jnp.exp((s_suf - peak) * SCALE)
-        w_new = jnp.exp((s_new - peak) * SCALE)
+        w_suf = jnp.exp2((s_suf - peak) * SCALE)
+        w_new = jnp.exp2((s_new - peak) * SCALE)
         both = dot(svt[k], w_suf.astype(BF16))
         numer = dot(vn[k].T.astype(BF16), w_new.astype(BF16))
         for i in range(per):
@@ -346,7 +348,8 @@
         )
 
     zb = max(1, min(R, 256 // L))
-    for k in range(kvw):
+
+    def every_row(k):
         cols = slice(k * HD, (k + 1) * HD)
         keys = jnp.concatenate(
             [
@@ -386,7 +389,7 @@
                 )
             s_pre = dot_nt(keys, jnp.concatenate(blocks, axis=0))
             peak = jnp.max(s_pre, axis=0, keepdims=True)
-            w_pre = jnp.exp((s_pre - peak) * SCALE)
+            w_pre = jnp.exp2((s_pre - peak) * SCALE)
             total = jnp.sum(w_pre, axis=0, keepdims=True)
             both = dot(vt[k], w_pre.astype(BF16))
             numer = jnp.zeros((HD, zb * L), F32)
@@ -413,7 +416,17 @@
                 cp.start()
                 sends.append(cp)
 
-    forwards = []
+    finish(0)
+    for cp in kv_remote:
+        cp.wait()
+    turn(1)
+    for k in range(1, kvw):
+        finish(k)
+    for k in range(kvw):
+        every_row(k)
+        own_rows(k)
+
+    forwards = {}
 
     def forward(k, o, place):
         rows = pl.ds(pl.multiple_of(place * rz, rz), rz)
@@ -422,7 +435,7 @@
             device_id={"seq": sib}, device_id_type=MESH,
         )
         cp.start()
-        forwards.append(cp)
+        forwards[k, o] = cp
 
     for k in range(kvw):
         for o in range(1, R):
@@ -438,7 +451,7 @@
         total = jnp.zeros((1, L), F32)
         numer = jnp.zeros((HD, L), F32)
         for (peak, part), piece in zip(stats, numers):
-            factor = jnp.exp((peak - top) * SCALE)
+            factor = jnp.exp2((peak - top) * SCALE)
             total = total + part * factor
             numer = numer + piece * factor
         share = (numer / total).T.astype(BF16)
@@ -466,18 +479,16 @@
             forward(k, o, source)
         oload[0, k].wait()
         total = total + dot(att[0, k], wo[0, k])
-    for cp in forwards:
-        cp.wait()
-    for k in range(kvw):
+        for o in range(R):
+            forwards[k, o].wait()
         oload[1, k].wait()
+        if k < kvw - 1:
+            total = total + dot(att[1, k], wo[1, k])
     nb, nc = dims["nb"], acc.shape[2]
     tps = {}
     for n in range(nb):
         cols = slice(n * nc, (n + 1) * nc)
-        piece = total[:, cols]
-        for k in range(kvw):
-            piece = piece + dot(att[1, k], wo[1, k, :, cols])
-        acc[n] = piece
+        acc[n] = total[:, cols] + dot(att[1, kvw - 1], wo[1, kvw - 1, :, cols])
         for o in range(1, T):
             dest = lax.rem(t + o, T)
             tps[n, o] = pltpu.make_async_remote_copy(

time: 47.1 us -> 46.3 us (0.983)
  Pallas kernels: 45.4 us -> 44.7 us
    pallas_call x1, Pallas kernels: 45.4 us -> 44.7 us  [body(): pl.pallas_call(functools.partial(kernel, dims), out_shape=jax.ShapeDtypeS...]
where the time goes in v3:
time: 46.3 us; the launch traced here: 46.1 us
  Pallas kernels  44.7 us (97%)
  local copies, waits for them, and re-layouts  1.47 us (3%)
    pallas_call x1, Pallas kernels, body(): pl.pallas_call(functools.partial(kernel, dims), out_shape=jax.ShapeDtypeS...  44.7 us
    unnamed x1, local copies, waits for them, and re-layouts  1.47 us

profile of v3, /device:TPU:0, one launch (start us, length us, event | category | flops | bytes accessed | tf_op | source)
XLA Modules:
  0.0 46.1 jit_solution(4953984395270428500)
XLA Ops:
  0.0 44.7 %shard_map.145 = bf16[32,1024]{1,0:T(8,128)(2,1)} custom-call(s32[8]{0:T(128)} %lens_ref.1, s32[8]{0:T(128)} %prompt_ref.1, f32[1,128]{1,0:T(1,128)} %constant.2.clone.freq_ref, bf16[4096]{0:T(1024)(128)(2,1)} %bq_ref.1, bf16[512]{0:T(512)(128)(2,1)} %bk_ref.1, bf16[512]{0:T(512)(128)(2,1)} %bv_ref.1, bf16[64,1024]{1,0:T(8,128)(2,1)} %hid_ref.1, ...), custom_call_target="tpu_custom_call" | custom-call | flops 1207959552 | bytes 25165824 | tf_op jit(solution)/shard_map/pallas_call | solution.py:550
  44.7 1.5 %copy.17 = bf16[32,1024]{1,0:T(8,128)(2,1)} copy(bf16[32,1024]{1,0:T(8,128)(2,1)} %shard_map.145) | data formatting | bytes 131072

commit v4 on v3

--- a/solution.py
+++ b/solution.py
@@ -72,6 +72,7 @@
     stin,
     att,
     acc,
+    accb,
     tin,
     bq,
     bk,
@@ -199,7 +200,8 @@
             src.at[:, :, pl.ds(kv_off(sib), W)], dst.at[1], sw_s.at[i], sw_r.at[i],
             device_id={"seq": sib}, device_id_type=MESH,
         )
-        cp.start()
+        if i < 2:
+            cp.start()
         kv_remote.append(cp)
     oload = {}
     for s, half in ((0, c), (1, sib)):
@@ -249,6 +251,8 @@
             )
             cp.start()
             sends.append(cp)
+    for cp in kv_remote[2:]:
+        cp.start()
     for src, dst in biases:
         dst[...] = src[...].astype(F32).reshape(dst.shape)
 
@@ -266,17 +270,17 @@
     def rotate(x):
         return x * cosine + pltpu.roll(x, HD // 2, 1) * sine
 
-    def turn(s):
+    def turn(src, dst, s):
+        count, length = src.shape[1], src.shape[2]
         for k in range(kvw):
             cols = slice(k * HD, (k + 1) * HD)
-            for p in range(prompts):
-                vt[k, p * HD : (p + 1) * HD, s * pre : (s + 1) * pre] = vb[s, p, :, cols].T
-            for p in range(per):
-                svt[k, p * HD : (p + 1) * HD, s * suf : (s + 1) * suf] = svb[s, p, :, cols].T
+            for p in range(count):
+                dst[k, p * HD : (p + 1) * HD, s * length : (s + 1) * length] = src[s, p, :, cols].T
 
     for cp in kv_local:
         cp.wait()
-    turn(0)
+    turn(vb, vt, 0)
+    turn(svb, svt, 0)
 
     def finish(k):
         for o in range(1, R):
@@ -417,14 +421,16 @@
                 sends.append(cp)
 
     finish(0)
-    for cp in kv_remote:
+    for cp in kv_remote[:2]:
         cp.wait()
-    turn(1)
+    turn(vb, vt, 1)
     for k in range(1, kvw):
         finish(k)
     for k in range(kvw):
         every_row(k)
-        own_rows(k)
+    for cp in kv_remote[2:]:
+        cp.wait()
+    turn(svb, svt, 1)
 
     forwards = {}
 
@@ -437,7 +443,7 @@
         cp.start()
         forwards[k, o] = cp
 
-    for k in range(kvw):
+    def combine(k):
         for o in range(1, R):
             arrived(lambda src, k=k: nin.at[k, src], nu_s.at[k, o], nu_r.at[k, o], o)
             arrived(lambda src, k=k: stin.at[k, src], st_s.at[k, o], st_r.at[k, o], o)
@@ -468,6 +474,10 @@
             cp.start()
             sends.append(cp)
         forward(k, 0, z)
+
+    for k in range(kvw):
+        own_rows(k)
+        combine(k)
 
     total = jnp.zeros((M, dims["nb"] * acc.shape[2]), F32)
     for k in range(kvw):
@@ -488,11 +498,13 @@
     tps = {}
     for n in range(nb):
         cols = slice(n * nc, (n + 1) * nc)
-        acc[n] = total[:, cols] + dot(att[1, kvw - 1], wo[1, kvw - 1, :, cols])
+        piece = total[:, cols] + dot(att[1, kvw - 1], wo[1, kvw - 1, :, cols])
+        acc[n] = piece
+        accb[n] = piece.astype(BF16)
         for o in range(1, T):
             dest = lax.rem(t + o, T)
             tps[n, o] = pltpu.make_async_remote_copy(
-                acc.at[n, pl.ds(pl.multiple_of(dest * mt, mt), mt)], tin.at[n, o - 1],
+                accb.at[n, pl.ds(pl.multiple_of(dest * mt, mt), mt)], tin.at[n, o - 1],
                 tp_s.at[n, o], tp_r.at[n, o], device_id={"tp": dest}, device_id_type=MESH,
             )
             tps[n, o].start()
@@ -500,7 +512,7 @@
         result = acc[n, pl.ds(pl.multiple_of(t * mt, mt), mt), :]
         for o in range(1, T):
             tps[n, o].wait()
-            result = result + tin[n, o - 1]
+            result = result + tin[n, o - 1].astype(F32)
         out_ref[:, n * nc : (n + 1) * nc] = result.astype(BF16)
     for cp in sends:
         cp.wait_send()
@@ -580,7 +592,8 @@
             pltpu.VMEM((kvw, R, 8, L), F32),
             pltpu.VMEM((S, kvw, M, gw), BF16),
             pltpu.VMEM((nb, M, N // nb), F32),
-            pltpu.VMEM((nb, max(T - 1, 1), M // T, N // nb), F32),
+            pltpu.VMEM((nb, M, N // nb), BF16),
+            pltpu.VMEM((nb, max(T - 1, 1), M // T, N // nb), BF16),
             pltpu.VMEM((1, q_heads * HD), F32),
             pltpu.VMEM((1, kvh * HD), F32),
             pltpu.VMEM((1, kvh * HD), F32),

time: 46.3 us -> 45 us (0.972)
  Pallas kernels: 44.7 us -> 43.3 us
    pallas_call x1, Pallas kernels: 44.7 us -> 43.3 us  [body(): pl.pallas_call(functools.partial(kernel, dims), out_shape=jax.ShapeDtypeS...]
where the time goes in v4:
time: 45 us; the launch traced here: 44.8 us
  Pallas kernels  43.3 us (96%)
  local copies, waits for them, and re-layouts  1.47 us (3%)
    pallas_call x1, Pallas kernels, body(): pl.pallas_call(functools.partial(kernel, dims), out_shape=jax.ShapeDtypeS...  43.3 us
    unnamed x1, local copies, waits for them, and re-layouts  1.47 us

profile of v4, /device:TPU:0, one launch (start us, length us, event | category | flops | bytes accessed | tf_op | source)
XLA Modules:
  0.0 44.8 jit_solution(4324698726958085438)
XLA Ops:
  0.0 43.3 %shard_map.145 = bf16[32,1024]{1,0:T(8,128)(2,1)} custom-call(s32[8]{0:T(128)} %lens_ref.1, s32[8]{0:T(128)} %prompt_ref.1, f32[1,128]{1,0:T(1,128)} %constant.2.clone.freq_ref, bf16[4096]{0:T(1024)(128)(2,1)} %bq_ref.1, bf16[512]{0:T(512)(128)(2,1)} %bk_ref.1, bf16[512]{0:T(512)(128)(2,1)} %bv_ref.1, bf16[64,1024]{1,0:T(8,128)(2,1)} %hid_ref.1, ...), custom_call_target="tpu_custom_call" | custom-call | flops 1207959552 | bytes 25165824 | tf_op jit(solution)/shard_map/pallas_call | solution.py:562
  43.3 1.5 %copy.17 = bf16[32,1024]{1,0:T(8,128)(2,1)} copy(bf16[32,1024]{1,0:T(8,128)(2,1)} %shard_map.145) | data formatting | bytes 131072
